TPU v7x, 32 devices: a whole 2x2x4 slice. The times are simulated.
32 devices in a mesh: kp: 8 (over z, x), kz: 4 (over y, core).
Axes of the slice: x: 2, y: 2, z: 4, core: 2. Of those that a mesh axis runs over, the one named last changes fastest.
Arguments:
- orbitals: bfloat16 [8, 4, 2, 64, 1024], P('kp', 'kz'), may hold values from -0.75 to 0.75
- trial_vectors: bfloat16 [8, 4, 2, 2, 1024], P('kp', 'kz'), may hold values from -6 to 6
- screened_table: bfloat16 [64, 2, 1024, 1024], P('kp', None, 'kz'), may hold values from -0.09375 to 0.09375
- shift_inplane: int32 [2], replicated, may hold values from -32 to 31
- shift_depth: int32 [2], replicated, may hold values from -16 to 15
- table_entry: int32 [2], replicated, may hold values from 0 to 63
Outputs:
- kernel_image: float32 [8, 4, 2, 2, 1024], P('kp', 'kz')
All inputs are finite; a program needn't handle non-finite values.
Results may differ from a plain program's by a relative error of at most 0.0049.
Values may be sent and summed in bfloat16 or wider, within the bound.
No kernel may reach another device: no remote copies, remote signals or barrier semaphores. Data moves between devices by JAX's collectives and lax.ppermute only.
A program may use at most 64 MiB of HBM per device.

v0:
```python
import jax
import jax.numpy as jnp
from jax import lax
from jax.sharding import PartitionSpec as P

NV = 32


def spread(shard, axis, root):
    mine = lax.axis_index(axis) == root
    return lax.psum(jnp.where(mine, shard, jnp.zeros_like(shard)), axis)


def passed_along(block, axis, distance):
    devices = range(lax.axis_size(axis))
    route = [((i - distance) % len(devices), i) for i in devices]
    return lax.ppermute(block, axis, route)


def pair_term(own_valence, own_conduction, next_valence, next_conduction, next_trial, screen_rows):
    valence_count = own_valence.shape[1]
    conduction_count = own_conduction.shape[1]
    row_span = own_conduction.shape[2]
    points = own_valence.shape[2]
    vector_count = next_trial.shape[0]
    trial_matrix = next_trial.reshape(vector_count, 2, conduction_count, valence_count)
    real_part = jnp.swapaxes(trial_matrix[:, 0], 1, 2)
    imag_part = jnp.swapaxes(trial_matrix[:, 1], 1, 2)
    upper_rows = jnp.concatenate([real_part, -imag_part], axis=2)
    lower_rows = jnp.concatenate([imag_part, real_part], axis=2)
    coeffs = jnp.stack([upper_rows, lower_rows], axis=1).reshape(
        vector_count * 2 * valence_count, 2 * conduction_count
    )
    amplitude = jnp.dot(
        coeffs,
        next_conduction.reshape(2 * conduction_count, row_span),
        preferred_element_type=jnp.float32,
    )
    amplitude = amplitude.astype(jnp.bfloat16).reshape(vector_count, 2, valence_count, row_span)
    partner_rows = next_valence.reshape(2 * valence_count, points)
    own_real = own_valence[0]
    own_imag = own_valence[1]
    valence_stack = jnp.concatenate(
        [
            jnp.concatenate([own_real, -own_imag], axis=1),
            jnp.concatenate([own_imag, own_real], axis=1),
        ],
        axis=0,
    )
    block = min(512, row_span)

    def one_vector(amplitude_pair):
        amp_real = amplitude_pair[0]
        amp_imag = amplitude_pair[1]

        def add_block(block_index, accumulated):
            left_factor = jnp.concatenate(
                [
                    jnp.concatenate([amp_real, amp_imag], axis=0),
                    jnp.concatenate([amp_imag, -amp_real], axis=0),
                ],
                axis=1,
            )
            expanded = lax.dot_general(
                left_factor,
                partner_rows,
                (((0,), (0,)), ((), ())),
                preferred_element_type=jnp.float32,
            )
            exp_real = expanded[:block]
            exp_imag = expanded[block:]
            w_real = screen_rows[0].astype(jnp.float32)
            w_imag = screen_rows[1].astype(jnp.float32)
            product = jnp.concatenate(
                [w_real * exp_real - w_imag * exp_imag, w_real * exp_imag + w_imag * exp_real],
                axis=1,
            ).astype(jnp.bfloat16)
            half_product = lax.dot_general(
                product, valence_stack, (((1,), (1,)), ((), ())), preferred_element_type=jnp.float32
            ).astype(jnp.bfloat16)
            half_real = half_product[:, :valence_count]
            half_imag = half_product[:, valence_count:]
            half_stack = jnp.concatenate(
                [
                    jnp.concatenate([half_real, half_imag], axis=1),
                    jnp.concatenate([half_imag, -half_real], axis=1),
                ],
                axis=0,
            )
            cond_cat = jnp.concatenate([own_conduction[0], own_conduction[1]], axis=1)
            return accumulated + jnp.dot(cond_cat, half_stack, preferred_element_type=jnp.float32)

        result = lax.fori_loop(
            0,
            row_span // block,
            add_block,
            jnp.zeros((conduction_count, 2 * valence_count), jnp.float32),
        )
        return jnp.stack(
            [result[:, :valence_count].reshape(-1), result[:, valence_count:].reshape(-1)]
        )

    return lax.map(one_vector, amplitude)


def shards(orbitals, trial_vectors, screened_table, shift_inplane, shift_depth, table_entry):
    slot_count = screened_table.shape[0]
    valence_count = NV
    plane_size = lax.axis_size("kp")
    depth_size = lax.axis_size("kz")
    plane_offsets = shift_inplane % plane_size
    depth_offsets = shift_depth % depth_size
    rows_list = []
    carried_list = []
    for transfer in range(2):
        target = table_entry[transfer]
        stored_slab = lax.dynamic_index_in_dim(
            screened_table, target % slot_count, 0, keepdims=False
        )
        rows_list.append(spread(stored_slab, "kp", target // slot_count))
        carried = (orbitals, trial_vectors)
        for bit_level in range((plane_size - 1).bit_length()):
            arrived = passed_along((carried[0], carried[1]), "kp", -(1 << bit_level))
            chosen = plane_offsets[transfer] // (1 << bit_level) % 2 == 1
            carried = (
                jnp.where(chosen, arrived[0], carried[0]),
                jnp.where(chosen, arrived[1], carried[1]),
            )
        carried_list.append(carried)
    first_pair = carried_list[0]
    second = carried_list[1]
    gathered = (
        lax.all_gather(orbitals[:, :, :, :valence_count], "kz", axis=1, tiled=True),
        lax.all_gather(first_pair[0][:, :, :, :valence_count], "kz", axis=1, tiled=True),
        lax.all_gather(second[0][:, :, :, :valence_count], "kz", axis=1, tiled=True),
        lax.all_gather(first_pair[1], "kz", axis=1, tiled=True),
        lax.all_gather(second[1], "kz", axis=1, tiled=True),
    )
    point_rows = (
        lax.all_to_all(
            orbitals[:, :, :, valence_count:], "kz", split_axis=4, concat_axis=1, tiled=True
        ),
        lax.all_to_all(
            first_pair[0][:, :, :, valence_count:], "kz", split_axis=4, concat_axis=1, tiled=True
        ),
        lax.all_to_all(
            second[0][:, :, :, valence_count:], "kz", split_axis=4, concat_axis=1, tiled=True
        ),
    )
    depth_first = depth_offsets[0]
    depth_second = depth_offsets[1]
    own_valence = gathered[0][0]
    own_conduction = point_rows[0][0]
    valence_first = jnp.roll(gathered[1][0], -depth_first, axis=0)
    valence_second = jnp.roll(gathered[2][0], -depth_second, axis=0)
    trial_first = jnp.roll(gathered[3][0], -depth_first, axis=0)
    trial_second = jnp.roll(gathered[4][0], -depth_second, axis=0)
    cond_first = jnp.roll(point_rows[1][0], -depth_first, axis=0)
    cond_second = jnp.roll(point_rows[2][0], -depth_second, axis=0)

    def one_point(point_items):
        return pair_term(
            point_items[0],
            point_items[1],
            point_items[2],
            point_items[3],
            point_items[4],
            rows_list[0],
        ) + pair_term(
            point_items[0],
            point_items[1],
            point_items[5],
            point_items[6],
            point_items[7],
            rows_list[1],
        )

    partials = lax.map(
        one_point,
        (
            own_valence,
            own_conduction,
            valence_first,
            cond_first,
            trial_first,
            valence_second,
            cond_second,
            trial_second,
        ),
    )
    summed = lax.psum_scatter(partials, "kz", scatter_dimension=0, tiled=True)
    return summed[None]


def solution(mesh):
    in_specs = (
        P("kp", "kz", None, None, None),
        P("kp", "kz", None, None, None),
        P("kp", None, "kz", None),
        P(),
        P(),
        P(),
    )
    out_specs = P("kp", "kz", None, None, None)
    return jax.shard_map(shards, mesh=mesh, in_specs=in_specs, out_specs=out_specs, check_vma=False)
```

profile of v0, /device:TPU:0, one launch (start us, length us, event | category | flops | bytes accessed | tf_op | source)
XLA Modules:
  0.0 253.5 jit_solution(17903872996071244630)
XLA Ops:
  7.8 6.0 %collective-permute-start.3 = (bf16[1,1,2,64,1024]{3,2,1,0,4:T(2,128)(2,1)S(1)}, bf16[1,1,2,64,1024]{3,2,1,0,4:T(2,128)(2,1)S(1)}, u32[]{:S(2)}, u32[]{:S(2)}) collective-permute-start(bf16[1,1,2,64,1024]{3,2,1,0,4:T(2,128)(2,1)S(1)} %copy.24), channel_id=1, source_target_pairs={{4,0},{8,4},{12,8},{16,12},{20,16},{24,20},{28,24},{0,28},{5,1},{9... | collective-permute-start | bytes 786440 | tf_op jit(solution)/shard_map/ppermute | solution.py:17
  16.2 3.3 %all-to-all-start.1 = ((bf16[4,2,8192]{2,1,0:T(2,128)(2,1)}), bf16[4,2,8192]{2,1,0:T(2,128)(2,1)S(1)}, u32[]{:S(2)}, u32[]{:S(2)}) async-start(bf16[4,2,8192]{2,1,0:T(2,128)(2,1)} %reshape.98), calls=%async_computation.1 | async-start | bytes 262144 | tf_op jit(solution)/shard_map/all_to_all | solution.py:140
  29.2 7.6 %all_gather.17 = bf16[1,4,2,32,1024]{4,3,2,0,1:T(8,128)(2,1)S(1)} all-gather(bf16[1,1,2,32,1024]{4,3,2,0,1:T(8,128)(2,1)S(1)} %slice.232), channel_id=1, replica_groups=mesh['kp'=8,'kz'=4] {'kz'}, dimensions={1}, use_global_device_ids=true | all-gather | bytes 655360 | tf_op jit(solution)/shard_map/all_gather | solution.py:133
  55.5 5.2 %all_gather.18 = bf16[1,4,2,2,1024]{4,3,2,0,1:T(2,128)(2,1)S(1)} all-gather(bf16[1,1,2,2,1024]{4,3,2,0,1:T(2,128)(2,1)S(1)} %broadcast_select_fusion.8), channel_id=1, replica_groups=mesh['kp'=8,'kz'=4] {'kz'}, dimensions={1}, use_global_device_ids=true | all-gather | bytes 40960 | tf_op jit(solution)/shard_map/all_gather | solution.py:137
  60.7 5.2 %all_gather.15 = bf16[1,4,2,2,1024]{4,3,2,0,1:T(2,128)(2,1)S(1)} all-gather(bf16[1,1,2,2,1024]{4,3,2,0,1:T(2,128)(2,1)S(1)} %broadcast_select_fusion.11), channel_id=1, replica_groups=mesh['kp'=8,'kz'=4] {'kz'}, dimensions={1}, use_global_device_ids=true | all-gather | bytes 40960 | tf_op jit(solution)/shard_map/all_gather | solution.py:136
  72.8 12.6 %collective-permute-done.4 = bf16[1,1,2,64,1024]{3,2,1,0,4:T(2,128)(2,1)S(1)} collective-permute-done((bf16[1,1,2,64,1024]{3,2,1,0,4:T(2,128)(2,1)S(1)}, bf16[1,1,2,64,1024]{3,2,1,0,4:T(2,128)(2,1)S(1)}, u32[]{:S(2)}, u32[]{:S(2)}) %collective-permute-start.4) | collective-permute-done | bytes 262176 | tf_op jit(solution)/shard_map/ppermute | solution.py:17
  85.9 3.8 %collective-permute-start.5 = (bf16[1,1,2,64,1024]{3,2,1,0,4:T(2,128)(2,1)S(1)}, bf16[1,1,2,64,1024]{3,2,1,0,4:T(2,128)(2,1)S(1)}, u32[]{:S(2)}, u32[]{:S(2)}) collective-permute-start(bf16[1,1,2,64,1024]{3,2,1,0,4:T(2,128)(2,1)S(1)} %broadcast_select_fusion.4), channel_id=1, source_target_pairs={{16,0},{20,4},{24,8},{28,12},{0,16},{4,20},{8,24},{12,28},{17,1},{... | collective-permute-start | bytes 786440 | tf_op jit(solution)/shard_map/ppermute | solution.py:17
  89.8 32.1 %collective-permute-done.9 = bf16[1,1,2,64,1024]{3,2,1,0,4:T(2,128)(2,1)S(1)} collective-permute-done((bf16[1,1,2,64,1024]{3,2,1,0,4:T(2,128)(2,1)S(1)}, bf16[1,1,2,64,1024]{3,2,1,0,4:T(2,128)(2,1)S(1)}, u32[]{:S(2)}, u32[]{:S(2)}) %collective-permute-start.9) | collective-permute-done | bytes 262176 | tf_op jit(solution)/shard_map/ppermute | solution.py:17
  124.9 3.3 %all-to-all-start.2 = ((bf16[4,2,8192]{2,1,0:T(2,128)(2,1)}), bf16[4,2,8192]{2,1,0:T(2,128)(2,1)S(1)}, u32[]{:S(2)}, u32[]{:S(2)}) async-start(bf16[4,2,8192]{2,1,0:T(2,128)(2,1)} %reshape.100), calls=%async_computation.2 | async-start | bytes 262144 | tf_op jit(solution)/shard_map/all_to_all | solution.py:146
  128.2 10.1 %collective-permute-done.5 = bf16[1,1,2,64,1024]{3,2,1,0,4:T(2,128)(2,1)S(1)} collective-permute-done((bf16[1,1,2,64,1024]{3,2,1,0,4:T(2,128)(2,1)S(1)}, bf16[1,1,2,64,1024]{3,2,1,0,4:T(2,128)(2,1)S(1)}, u32[]{:S(2)}, u32[]{:S(2)}) %collective-permute-start.5) | collective-permute-done | bytes 262176 | tf_op jit(solution)/shard_map/ppermute | solution.py:17
  141.3 7.1 %all_gather.19 = bf16[1,4,2,32,1024]{4,3,2,0,1:T(8,128)(2,1)S(1)} all-gather(bf16[1,1,2,32,1024]{4,3,2,0,1:T(8,128)(2,1)S(1)} %copy.34), channel_id=1, replica_groups=mesh['kp'=8,'kz'=4] {'kz'}, dimensions={1}, use_global_device_ids=true | all-gather | bytes 655360 | tf_op jit(solution)/shard_map/all_gather | solution.py:135
  148.4 7.5 %all_gather.16 = bf16[1,4,2,32,1024]{4,3,2,0,1:T(8,128)(2,1)S(1)} all-gather(bf16[1,1,2,32,1024]{4,3,2,0,1:T(8,128)(2,1)S(1)} %copy.27), channel_id=1, replica_groups=mesh['kp'=8,'kz'=4] {'kz'}, dimensions={1}, use_global_device_ids=true | all-gather | bytes 655360 | tf_op jit(solution)/shard_map/all_gather | solution.py:134
  156.8 3.3 %all-to-all-start = ((bf16[4,2,8192]{2,1,0:T(2,128)(2,1)}), bf16[4,2,8192]{2,1,0:T(2,128)(2,1)S(1)}, u32[]{:S(2)}, u32[]{:S(2)}) async-start(bf16[4,2,8192]{2,1,0:T(2,128)(2,1)} %reshape.96), calls=%async_computation | async-start | bytes 262144 | tf_op jit(solution)/shard_map/all_to_all | solution.py:143
  166.7 4.1 %all-reduce.7.cloned.1.call-done = (bf16[2,256,1024]{2,1,0:T(8,128)(2,1)}, bf16[2,256,1024]{2,1,0:T(8,128)(2,1)}) async-done(((bf16[2,256,1024]{2,1,0:T(8,128)(2,1)}, bf16[2,256,1024]{2,1,0:T(8,128)(2,1)}), (bf16[2,256,1024]{2,1,0:T(8,128)(2,1)}, bf16[2,256,1024]{2,1,0:T(8,128)(2,1)})) %all-reduce.7.cloned.1.call-update) | async-done | bytes 2097168 | tf_op jit(solution)/shard_map/psum | solution.py:11
  170.8 42.9 %while.44 = (s32[]{:T(128)}, f32[4,2,2,1024]{3,2,1,0:T(2,128)}, bf16[4,2,2,1024]{3,2,1,0:T(2,128)(2,1)S(1)}, bf16[4,2,32,256]{3,2,1,0:T(8,128)(2,1)}, bf16[4,2,3...) while((s32[]{:T(128)}, f32[4,2,2,1024]{3,2,1,0:T(2,128)}, ...), condition=%wide.region_7.11_spmd, body=%wide.region_2.10_spmd.sunk | while | flops 292745216 | bytes 26813664 | solution.py:178
  173.2 3.6 %while.46 = (s32[]{:T(128)}, f32[2,2,1024]{2,1,0:T(2,128)S(1)}, bf16[2,256,1024]{2,1,0:T(8,128)(2,1)S(1)}, bf16[2,2,32,256]{3,2,1,0:T(8,128)(2,1)S(1)}, bf16[64,...) while((s32[]{:T(128)}, f32[2,2,1024]{2,1,0:T(2,128)S(1)}, ...), condition=%wide.region_6.9_spmd, body=%wide.region_5.8_spmd.sunk | while | flops 141527040 | bytes 8118401 | solution.py:103
  177.3 3.6 %while.45 = (s32[]{:T(128)}, f32[2,2,1024]{2,1,0:T(2,128)S(1)}, bf16[2,256,1024]{2,1,0:T(8,128)(2,1)S(1)}, bf16[2,2,32,256]{3,2,1,0:T(8,128)(2,1)S(1)}, bf16[64,...) while((s32[]{:T(128)}, f32[2,2,1024]{2,1,0:T(2,128)S(1)}, ...), condition=%wide.region_4.7_spmd, body=%wide.region_3.6_spmd.sunk | while | flops 141527040 | bytes 8118401 | solution.py:103
  183.9 3.6 %while.46 = (s32[]{:T(128)}, f32[2,2,1024]{2,1,0:T(2,128)S(1)}, bf16[2,256,1024]{2,1,0:T(8,128)(2,1)S(1)}, bf16[2,2,32,256]{3,2,1,0:T(8,128)(2,1)S(1)}, bf16[64,...) while((s32[]{:T(128)}, f32[2,2,1024]{2,1,0:T(2,128)S(1)}, ...), condition=%wide.region_6.9_spmd, body=%wide.region_5.8_spmd.sunk | while | flops 141527040 | bytes 8118401 | solution.py:103
  188.0 3.6 %while.45 = (s32[]{:T(128)}, f32[2,2,1024]{2,1,0:T(2,128)S(1)}, bf16[2,256,1024]{2,1,0:T(8,128)(2,1)S(1)}, bf16[2,2,32,256]{3,2,1,0:T(8,128)(2,1)S(1)}, bf16[64,...) while((s32[]{:T(128)}, f32[2,2,1024]{2,1,0:T(2,128)S(1)}, ...), condition=%wide.region_4.7_spmd, body=%wide.region_3.6_spmd.sunk | while | flops 141527040 | bytes 8118401 | solution.py:103
  194.6 3.6 %while.46 = (s32[]{:T(128)}, f32[2,2,1024]{2,1,0:T(2,128)S(1)}, bf16[2,256,1024]{2,1,0:T(8,128)(2,1)S(1)}, bf16[2,2,32,256]{3,2,1,0:T(8,128)(2,1)S(1)}, bf16[64,...) while((s32[]{:T(128)}, f32[2,2,1024]{2,1,0:T(2,128)S(1)}, ...), condition=%wide.region_6.9_spmd, body=%wide.region_5.8_spmd.sunk | while | flops 141527040 | bytes 8118401 | solution.py:103
  198.7 3.6 %while.45 = (s32[]{:T(128)}, f32[2,2,1024]{2,1,0:T(2,128)S(1)}, bf16[2,256,1024]{2,1,0:T(8,128)(2,1)S(1)}, bf16[2,2,32,256]{3,2,1,0:T(8,128)(2,1)S(1)}, bf16[64,...) while((s32[]{:T(128)}, f32[2,2,1024]{2,1,0:T(2,128)S(1)}, ...), condition=%wide.region_4.7_spmd, body=%wide.region_3.6_spmd.sunk | while | flops 141527040 | bytes 8118401 | solution.py:103
  205.3 3.6 %while.46 = (s32[]{:T(128)}, f32[2,2,1024]{2,1,0:T(2,128)S(1)}, bf16[2,256,1024]{2,1,0:T(8,128)(2,1)S(1)}, bf16[2,2,32,256]{3,2,1,0:T(8,128)(2,1)S(1)}, bf16[64,...) while((s32[]{:T(128)}, f32[2,2,1024]{2,1,0:T(2,128)S(1)}, ...), condition=%wide.region_6.9_spmd, body=%wide.region_5.8_spmd.sunk | while | flops 141527040 | bytes 8118401 | solution.py:103
  209.4 3.6 %while.45 = (s32[]{:T(128)}, f32[2,2,1024]{2,1,0:T(2,128)S(1)}, bf16[2,256,1024]{2,1,0:T(8,128)(2,1)S(1)}, bf16[2,2,32,256]{3,2,1,0:T(8,128)(2,1)S(1)}, bf16[64,...) while((s32[]{:T(128)}, f32[2,2,1024]{2,1,0:T(2,128)S(1)}, ...), condition=%wide.region_4.7_spmd, body=%wide.region_3.6_spmd.sunk | while | flops 141527040 | bytes 8118401 | solution.py:103
  214.4 30.3 %all-reduce.5.cloned.1.call-done = f32[4,2,2,1024]{3,2,1,0:T(2,128)} async-done(((f32[4,2,2,1024]{3,2,1,0:T(2,128)}), f32[4,2,2,1024]{3,2,1,0:T(2,128)}) %all-reduce.5.cloned.1.call-update) | async-done | bytes 65552
  (367 shorter events, 84.9 us)
Async XLA Ops:
  6.5 13.0 %copy-start.4 = (s32[2]{0:T(128)S(1)}, s32[2]{0:T(128)}, u32[]{:S(2)}) copy-start(s32[2]{0:T(128)} %param.23) | copy-start | bytes 28
  7.8 43.9 %collective-permute-start.3 = (bf16[1,1,2,64,1024]{3,2,1,0,4:T(2,128)(2,1)S(1)}, bf16[1,1,2,64,1024]{3,2,1,0,4:T(2,128)(2,1)S(1)}, u32[]{:S(2)}, u32[]{:S(2)}) collective-permute-start(bf16[1,1,2,64,1024]{3,2,1,0,4:T(2,128)(2,1)S(1)} %copy.24), channel_id=1, source_target_pairs={{4,0},{8,4},{12,8},{16,12},{20,16},{24,20},{28,24},{0,28},{5,1},{9... | collective-permute-start | bytes 786440 | tf_op jit(solution)/shard_map/ppermute | solution.py:17
  13.8 27.7 %collective-permute-start = (bf16[1,1,2,2,1024]{4,3,2,0,1:T(2,128)(2,1)}, bf16[1,1,2,2,1024]{4,3,2,0,1:T(2,128)(2,1)S(1)}, u32[]{:S(2)}, u32[]{:S(2)}) collective-permute-start(bf16[1,1,2,2,1024]{4,3,2,0,1:T(2,128)(2,1)} %bitcast.238), channel_id=1, source_target_pairs={{4,0},{8,4},{12,8},{16,12},{20,16},{24,20},{28,24},{0,28},{5,1},{9... | collective-permute-start | bytes 24584 | tf_op jit(solution)/shard_map/ppermute | solution.py:17
  16.2 49.9 %all-to-all-start.1 = ((bf16[4,2,8192]{2,1,0:T(2,128)(2,1)}), bf16[4,2,8192]{2,1,0:T(2,128)(2,1)S(1)}, u32[]{:S(2)}, u32[]{:S(2)}) async-start(bf16[4,2,8192]{2,1,0:T(2,128)(2,1)} %reshape.98), calls=%async_computation.1 | async-start | bytes 262144 | tf_op jit(solution)/shard_map/all_to_all | solution.py:140
  19.5 151.3 %all-reduce.7.cloned.1.call-start = ((), (), s32[]{:S(2)}) async-start(), calls=%async_computation.4 | async-start | bytes 4194304 | tf_op jit(solution)/shard_map/psum | solution.py:11
  28.3 8.6 %copy-start.5 = (s32[2]{0:T(128)S(1)}, s32[2]{0:T(128)}, u32[]{:S(2)}) copy-start(s32[2]{0:T(128)} %param.22) | copy-start | bytes 28
  28.3 8.6 %copy-start.6 = (s32[2]{0:T(128)S(1)}, s32[2]{0:T(128)}, u32[]{:S(2)}) copy-start(s32[2]{0:T(128)} %param.21) | copy-start | bytes 28
  28.3 13.3 %copy-start.3 = (bf16[1,1,2,2,1024]{4,3,2,1,0:T(2,128)(2,1)S(1)}, bf16[1,1,2,2,1024]{4,3,2,1,0:T(2,128)(2,1)}, u32[]{:S(2)}) copy-start(bf16[1,1,2,2,1024]{4,3,2,1,0:T(2,128)(2,1)} %param.19) | copy-start | bytes 24580
  41.6 4.9 %collective-permute-start.6 = (bf16[1,1,2,2,1024]{4,3,2,0,1:T(2,128)(2,1)S(1)}, bf16[1,1,2,2,1024]{4,3,2,0,1:T(2,128)(2,1)S(1)}, u32[]{:S(2)}, u32[]{:S(2)}) collective-permute-start(bf16[1,1,2,2,1024]{4,3,2,0,1:T(2,128)(2,1)S(1)} %get-tuple-element.405), channel_id=1, source_target_pairs={{8,0},{12,4},{16,8},{20,12},{24,16},{28,20},{0,24},{4,28},{9,1},{1... | collective-permute-start | bytes 24584 | tf_op jit(solution)/shard_map/ppermute | solution.py:17
  45.5 4.8 %collective-permute-start.1 = (bf16[1,1,2,2,1024]{4,3,2,0,1:T(2,128)(2,1)S(1)}, bf16[1,1,2,2,1024]{4,3,2,0,1:T(2,128)(2,1)S(1)}, u32[]{:S(2)}, u32[]{:S(2)}) collective-permute-start(bf16[1,1,2,2,1024]{4,3,2,0,1:T(2,128)(2,1)S(1)} %get-tuple-element.406), channel_id=1, source_target_pairs={{8,0},{12,4},{16,8},{20,12},{24,16},{28,20},{0,24},{4,28},{9,1},{1... | collective-permute-start | bytes 24584 | tf_op jit(solution)/shard_map/ppermute | solution.py:17
  46.5 5.2 %collective-permute-start.7 = (bf16[1,1,2,2,1024]{4,3,2,0,1:T(2,128)(2,1)S(1)}, bf16[1,1,2,2,1024]{4,3,2,0,1:T(2,128)(2,1)S(1)}, u32[]{:S(2)}, u32[]{:S(2)}) collective-permute-start(bf16[1,1,2,2,1024]{4,3,2,0,1:T(2,128)(2,1)S(1)} %broadcast_select_fusion.7), channel_id=1, source_target_pairs={{16,0},{20,4},{24,8},{28,12},{0,16},{4,20},{8,24},{12,28},{17,1},{... | collective-permute-start | bytes 24584 | tf_op jit(solution)/shard_map/ppermute | solution.py:17
  50.3 5.1 %collective-permute-start.2 = (bf16[1,1,2,2,1024]{4,3,2,0,1:T(2,128)(2,1)S(1)}, bf16[1,1,2,2,1024]{4,3,2,0,1:T(2,128)(2,1)S(1)}, u32[]{:S(2)}, u32[]{:S(2)}) collective-permute-start(bf16[1,1,2,2,1024]{4,3,2,0,1:T(2,128)(2,1)S(1)} %broadcast_select_fusion.10), channel_id=1, source_target_pairs={{16,0},{20,4},{24,8},{28,12},{0,16},{4,20},{8,24},{12,28},{17,1},{... | collective-permute-start | bytes 24584 | tf_op jit(solution)/shard_map/ppermute | solution.py:17
  52.6 16.6 %collective-permute-start.8 = (bf16[1,1,2,64,1024]{3,2,1,0,4:T(2,128)(2,1)S(1)}, bf16[1,1,2,64,1024]{3,2,1,0,4:T(2,128)(2,1)S(1)}, u32[]{:S(2)}, u32[]{:S(2)}) collective-permute-start(bf16[1,1,2,64,1024]{3,2,1,0,4:T(2,128)(2,1)S(1)} %get-tuple-element.399), channel_id=1, source_target_pairs={{8,0},{12,4},{16,8},{20,12},{24,16},{28,20},{0,24},{4,28},{9,1},{1... | collective-permute-start | bytes 786440 | tf_op jit(solution)/shard_map/ppermute | solution.py:17
  66.8 18.6 %collective-permute-start.4 = (bf16[1,1,2,64,1024]{3,2,1,0,4:T(2,128)(2,1)S(1)}, bf16[1,1,2,64,1024]{3,2,1,0,4:T(2,128)(2,1)S(1)}, u32[]{:S(2)}, u32[]{:S(2)}) collective-permute-start(bf16[1,1,2,64,1024]{3,2,1,0,4:T(2,128)(2,1)S(1)} %get-tuple-element.400), channel_id=1, source_target_pairs={{8,0},{12,4},{16,8},{20,12},{24,16},{28,20},{0,24},{4,28},{9,1},{1... | collective-permute-start | bytes 786440 | tf_op jit(solution)/shard_map/ppermute | solution.py:17
  69.8 52.1 %collective-permute-start.9 = (bf16[1,1,2,64,1024]{3,2,1,0,4:T(2,128)(2,1)S(1)}, bf16[1,1,2,64,1024]{3,2,1,0,4:T(2,128)(2,1)S(1)}, u32[]{:S(2)}, u32[]{:S(2)}) collective-permute-start(bf16[1,1,2,64,1024]{3,2,1,0,4:T(2,128)(2,1)S(1)} %broadcast_select_fusion.1), channel_id=1, source_target_pairs={{16,0},{20,4},{24,8},{28,12},{0,16},{4,20},{8,24},{12,28},{17,1},{... | collective-permute-start | bytes 786440 | tf_op jit(solution)/shard_map/ppermute | solution.py:17
  85.9 52.4 %collective-permute-start.5 = (bf16[1,1,2,64,1024]{3,2,1,0,4:T(2,128)(2,1)S(1)}, bf16[1,1,2,64,1024]{3,2,1,0,4:T(2,128)(2,1)S(1)}, u32[]{:S(2)}, u32[]{:S(2)}) collective-permute-start(bf16[1,1,2,64,1024]{3,2,1,0,4:T(2,128)(2,1)S(1)} %broadcast_select_fusion.4), channel_id=1, source_target_pairs={{16,0},{20,4},{24,8},{28,12},{0,16},{4,20},{8,24},{12,28},{17,1},{... | collective-permute-start | bytes 786440 | tf_op jit(solution)/shard_map/ppermute | solution.py:17
  124.9 31.9 %all-to-all-start.2 = ((bf16[4,2,8192]{2,1,0:T(2,128)(2,1)}), bf16[4,2,8192]{2,1,0:T(2,128)(2,1)S(1)}, u32[]{:S(2)}, u32[]{:S(2)}) async-start(bf16[4,2,8192]{2,1,0:T(2,128)(2,1)} %reshape.100), calls=%async_computation.2 | async-start | bytes 262144 | tf_op jit(solution)/shard_map/all_to_all | solution.py:146
  156.8 7.9 %all-to-all-start = ((bf16[4,2,8192]{2,1,0:T(2,128)(2,1)}), bf16[4,2,8192]{2,1,0:T(2,128)(2,1)S(1)}, u32[]{:S(2)}, u32[]{:S(2)}) async-start(bf16[4,2,8192]{2,1,0:T(2,128)(2,1)} %reshape.96), calls=%async_computation | async-start | bytes 262144 | tf_op jit(solution)/shard_map/all_to_all | solution.py:143
  160.2 84.5 %all-reduce.5.cloned.1.call-start = ((), (), s32[]{:S(2)}) async-start(), calls=%async_computation.3 | async-start | bytes 131072
  170.8 42.9 %copy-start.7 = (u32[32]{0:T(128)S(1)}, u32[32]{0:T(128)}, u32[]{:S(2)}) copy-start(u32[32]{0:T(128)} %constant.259) | copy-start | bytes 388
  173.2 4.1 %copy-start = (bf16[2,256,1024]{2,1,0:T(8,128)(2,1)S(1)}, bf16[2,256,1024]{2,1,0:T(8,128)(2,1)}, u32[]{:S(2)}) copy-start(bf16[2,256,1024]{2,1,0:T(8,128)(2,1)} %get-tuple-element.786) | copy-start | bytes 3145732 | tf_op jit(solution)/shard_map/while
  183.9 4.1 %copy-start = (bf16[2,256,1024]{2,1,0:T(8,128)(2,1)S(1)}, bf16[2,256,1024]{2,1,0:T(8,128)(2,1)}, u32[]{:S(2)}) copy-start(bf16[2,256,1024]{2,1,0:T(8,128)(2,1)} %get-tuple-element.786) | copy-start | bytes 3145732 | tf_op jit(solution)/shard_map/while
  194.6 4.1 %copy-start = (bf16[2,256,1024]{2,1,0:T(8,128)(2,1)S(1)}, bf16[2,256,1024]{2,1,0:T(8,128)(2,1)}, u32[]{:S(2)}) copy-start(bf16[2,256,1024]{2,1,0:T(8,128)(2,1)} %get-tuple-element.786) | copy-start | bytes 3145732 | tf_op jit(solution)/shard_map/while
  205.3 4.1 %copy-start = (bf16[2,256,1024]{2,1,0:T(8,128)(2,1)S(1)}, bf16[2,256,1024]{2,1,0:T(8,128)(2,1)}, u32[]{:S(2)}) copy-start(bf16[2,256,1024]{2,1,0:T(8,128)(2,1)} %get-tuple-element.786) | copy-start | bytes 3145732 | tf_op jit(solution)/shard_map/while
  (5 other events, 10.4 us)
Sparse Core Ops, SparseCore 0:
  28.4 142.3 all-reduce.6
  213.8 30.8 all-reduce.4
where the time goes:
time: 254 us
  waiting for transfers between devices  95.8 us (38%)
  blocking collectives  32.5 us (13%)
  starting transfers between devices  31.8 us (13%)
  local copies, waits for them, and re-layouts  28.3 us (11%)
  between operations  25.6 us (10%)
  other arithmetic  20.6 us (8%)
  matrix products  17.4 us (7%)
    ppermute x10, waiting for transfers between devices, passed_along(): return lax.ppermute(block, axis, route)  58.4 us
    unnamed x3, waiting for transfers between devices  30.3 us
    ppermute x10, starting transfers between devices, passed_along(): return lax.ppermute(block, axis, route)  21.7 us
    unnamed x21, local copies, waits for them, and re-layouts  7.76 us
    all_gather x1, blocking collectives, shards(): lax.all_gather(orbitals[:, :, :, :valence_count], 'kz', axis=1, tiled=True)  7.61 us
    all_gather x1, blocking collectives, shards(): lax.all_gather(first_pair[0][:, :, :, :valence_count], 'kz', axis=1, tile...  7.46 us
    dynamic_slice x12, local copies, waits for them, and re-layouts, shards(): lax.map(one_point, (own_valence, own_conduction, valence_first, cond_firs...  7.31 us
    dot_general x16, matrix products, add_block(): lax.dot_general(left_factor, partner_rows, (((0,), (0,)), ((), ())), pref...  7.19 us
  transfers between devices with their start and end apart: 15, of which 11 were waited for; matrix products, arithmetic and copies ran while one was open for 8% of the time, Pallas kernels for 0%

commit v1 on v0

v1 whole, which is shorter than its diff:
```python
import functools

import jax
import jax.numpy as jnp
from jax import lax
from jax.experimental import pallas as pl
from jax.experimental.pallas import tpu as pltpu
from jax.sharding import PartitionSpec as P

NV = 32
PAIR = 2
F32 = jnp.float32
BF16 = jnp.bfloat16


def swapped(block, axis):
    return lax.ppermute(block, axis, [(i, i ^ 1) for i in range(lax.axis_size(axis))])


def passed_along(block, distance):
    size = lax.axis_size("kp")
    return lax.ppermute(block, "kp", [(i, (i + PAIR * distance) % size) for i in range(size)])


def packed(orbitals, trial_vectors, planes, depths):
    bands = orbitals.shape[1]
    points = orbitals.shape[2]
    vectors = trial_vectors.shape[0]
    conduction = bands - NV
    half = points // (planes * PAIR)
    rows = points // (depths * PAIR * PAIR)
    valence = orbitals[:, :NV].reshape(2 * NV, planes, 1, 1, PAIR, half)
    valence = valence.transpose(1, 2, 3, 4, 0, 5)
    cond = orbitals[:, NV:].reshape(2 * conduction, 1, depths, PAIR, PAIR, rows)
    cond = cond.transpose(1, 4, 2, 3, 0, 5)
    trial = trial_vectors.reshape(vectors, 2, conduction, NV).transpose(2, 0, 1, 3)
    width = vectors * 2 * NV
    trial = trial.reshape(conduction, width)
    lead = (planes, PAIR, depths, PAIR)
    parts = [
        jnp.broadcast_to(valence, lead + valence.shape[4:]),
        jnp.broadcast_to(cond, lead + cond.shape[4:]),
    ]
    trial = trial.reshape(1, 1, 1, PAIR, conduction // PAIR, width)
    trial = jnp.broadcast_to(trial, lead + trial.shape[4:])
    count = planes * PAIR * depths * PAIR
    if half == rows == width:
        return (jnp.concatenate(parts + [trial], axis=4).reshape(count, -1, half),)
    return tuple(part.reshape((count,) + part.shape[4:]) for part in parts + [trial])


def screen_blocks(table, table_entry, lanes, planes, depths):
    slots, _, span, points = table.shape
    plane = lax.axis_index("kp") // PAIR
    side = lax.axis_index("kp") % PAIR
    core = lax.axis_index("kz") % PAIR
    rows = span // PAIR
    columns = points // planes
    half = columns // PAIR
    owner = table_entry // slots
    slot = table_entry % slots
    owner_plane = owner // PAIR
    owner_side = owner % PAIR
    mine = lax.axis_index("kp")
    if lanes == 1:
        first = plane == owner_plane[0]
        choices = [
            (
                jnp.where(mine == owner[0], slot[0], slot[1]),
                jnp.where(first, owner_side[0], owner_side[1]),
            )
        ]
    else:
        choices = [(slot[t], owner_side[t]) for t in range(2)]

    def cut(which, part):
        return lax.dynamic_slice(table, (which, 0, part * rows, 0), (1, 2, rows, points))[0]

    held = []
    for which, source_side in choices:
        arrived = swapped(cut(which, 1 - side), "kp")
        held.append(jnp.where(source_side == side, cut(which, side), arrived))
    held = jnp.stack(held)

    def columns_of(target):
        start = target * columns
        near = lax.dynamic_slice_in_dim(held, start + core * half, half, 3)
        far = lax.dynamic_slice_in_dim(held, start + (1 - core) * half, half, 3)
        return jnp.concatenate([near, far], axis=3)

    blocks = [columns_of(plane)]
    for distance in range(1, planes):
        blocks.append(passed_along(columns_of((plane + distance) % planes), distance))
    blocks = jnp.stack(blocks)
    picked = []
    for t in range(2):
        distance = (plane - owner_plane[t]) % planes
        lane = 0 if lanes == 1 else t
        picked.append(lax.dynamic_index_in_dim(blocks, distance, 0, keepdims=False)[lane])
    return jnp.stack(picked)


def compute(
    core_ref, own_ref, near_ref, far_ref, cond_ref, tri_near_ref, tri_far_ref, screen_ref,
    out_ref, wide_ref, sums_ref,
):
    count, pair_bands, rows = cond_ref.shape
    conduction = pair_bands // 2
    width = out_ref.shape[2]
    vectors = width // (2 * NV)
    wide_ref[...] = screen_ref[...].astype(F32)
    sums_ref[...] = jnp.zeros_like(sums_ref)
    lane = lax.broadcasted_iota(jnp.int32, (conduction, width), 1)
    low = lane % (2 * NV) < NV
    vector_of = lane // (2 * NV)
    core = core_ref[0]

    def turned(x):
        return jnp.where(low, -pltpu.roll(x, width - NV, 1), pltpu.roll(x, NV, 1))

    def valence_of(k):
        return jnp.concatenate([near_ref[k], far_ref[k]], axis=1)

    def step(partner, carry):
        valence = valence_of(partner)
        near = tri_near_ref[partner].astype(F32)
        far = tri_far_ref[partner].astype(F32)
        trial = jnp.concatenate(
            [jnp.where(core == 0, near, far), jnp.where(core == 0, far, near)], axis=0
        )
        turn = turned(trial)
        coeffs = jnp.concatenate(
            [
                jnp.concatenate([trial, -turn], axis=1),
                jnp.concatenate([turn, trial], axis=1),
            ],
            axis=0,
        ).astype(BF16)
        amplitude = lax.dot_general(
            cond_ref[partner], coeffs, (((0,), (0,)), ((), ())), preferred_element_type=F32
        ).astype(BF16)
        left = jnp.concatenate([amplitude[:, :width], amplitude[:, width:]], axis=0)
        screened = [[], []]
        blank = jnp.zeros_like(valence)
        for n in range(vectors):
            right = jnp.concatenate([valence if m == n else blank for m in range(vectors)], axis=0)
            expanded = jnp.dot(left, right, preferred_element_type=F32)
            real = expanded[:rows]
            imag = expanded[rows:]
            for t in range(2):
                w_real = wide_ref[t, 0]
                w_imag = wide_ref[t, 1]
                screened[t].append(
                    (
                        (w_real * real - w_imag * imag).astype(BF16),
                        (w_real * imag + w_imag * real).astype(BF16),
                    )
                )
        for t in range(2):
            own = own_ref[t, partner]
            mine = valence_of(own)
            cross = jnp.concatenate([-mine[NV:], mine[:NV]], axis=0)
            copies = [mine] * vectors
            crosses = [cross] * vectors
            s_real = jnp.concatenate([s[0] for s in screened[t]], axis=0)
            s_imag = jnp.concatenate([s[1] for s in screened[t]], axis=0)
            contract = (((1,), (1,)), ((), ()))
            half = lax.dot_general(
                s_real, jnp.concatenate(copies, axis=0), contract, preferred_element_type=F32
            ) + lax.dot_general(
                s_imag, jnp.concatenate(crosses, axis=0), contract, preferred_element_type=F32
            )
            half = half.astype(BF16)
            upper = jnp.zeros((conduction, width), F32)
            lower = jnp.zeros((conduction, width), F32)
            for n in range(vectors):
                product = jnp.dot(
                    cond_ref[own], half[n * rows : (n + 1) * rows], preferred_element_type=F32
                )
                upper = jnp.where(vector_of == n, product[:conduction], upper)
                lower = jnp.where(vector_of == n, product[conduction:], lower)
            sums_ref[own] += upper - turned(lower)
        return carry

    lax.fori_loop(0, count, step, 0)
    out_ref[...] = sums_ref[...].astype(BF16)


def shards(orbitals, trial_vectors, screened_table, shift_inplane, shift_depth, table_entry):
    plane_size = lax.axis_size("kp")
    depth_size = lax.axis_size("kz")
    planes = plane_size // PAIR
    depths = depth_size // PAIR
    count = plane_size * depth_size
    vectors = trial_vectors.shape[2]
    conduction = orbitals.shape[3] - NV
    axes = ("kp", "kz")
    own_orbitals = orbitals[0, 0]
    own_trial = trial_vectors[0, 0]
    ids = jnp.arange(count, dtype=jnp.int32)
    own = jnp.stack(
        [
            (ids // depth_size - shift_inplane[t]) % plane_size * depth_size
            + (ids % depth_size - shift_depth[t]) % depth_size
            for t in range(2)
        ]
    ).astype(jnp.int32)
    core = (lax.axis_index("kz") % PAIR).astype(jnp.int32).reshape(1)

    def run(lanes):
        sent = packed(own_orbitals, own_trial, planes, depths)
        came = [lax.all_to_all(part, axes, 0, 0, tiled=True) for part in sent]
        if len(came) == 1:
            both = came[0]
            near = both[:, : 2 * NV]
            cond = both[:, 2 * NV : 2 * (NV + conduction)]
            tri_near = both[:, 2 * (NV + conduction) :]
        else:
            near, cond, tri_near = came
        far, tri_far = swapped((near, tri_near), "kz")
        screen = screen_blocks(screened_table, table_entry, lanes, planes, depths)
        width = vectors * 2 * NV
        vmem = pl.BlockSpec(memory_space=pltpu.VMEM)
        smem = pl.BlockSpec(memory_space=pltpu.SMEM)
        partial = pl.pallas_call(
            compute,
            out_shape=jax.ShapeDtypeStruct((count, conduction, width), BF16),
            in_specs=[smem, smem] + [vmem] * 6,
            out_specs=vmem,
            scratch_shapes=[
                pltpu.VMEM(screen.shape, F32),
                pltpu.VMEM((count, conduction, width), F32),
            ],
            compiler_params=pltpu.CompilerParams(vmem_limit_bytes=56 << 20),
        )(core, own, near, far, cond, tri_near, tri_far, screen)
        terms = lax.all_to_all(partial, axes, 0, 0, tiled=True)
        image = jnp.sum(terms.astype(F32), axis=0)
        image = image.reshape(conduction, vectors, 2, NV).transpose(1, 2, 0, 3)
        return image.reshape(1, 1, vectors, 2, conduction * NV)

    owner_plane = table_entry // screened_table.shape[0] // PAIR
    return lax.cond(
        owner_plane[0] == owner_plane[1],
        functools.partial(run, 2),
        functools.partial(run, 1),
    )


def solution(mesh):
    in_specs = (
        P("kp", "kz", None, None, None),
        P("kp", "kz", None, None, None),
        P("kp", None, "kz", None),
        P(),
        P(),
        P(),
    )
    out_specs = P("kp", "kz", None, None, None)
    return jax.shard_map(shards, mesh=mesh, in_specs=in_specs, out_specs=out_specs, check_vma=False)
```

time: 254 us -> 143 us (0.56)
  waiting for transfers between devices: 95.8 us -> 42.7 us
  Pallas kernels: 0 us -> 39.2 us
  between operations: 25.6 us -> 1.31 us
  local copies, waits for them, and re-layouts: 28.3 us -> 10.8 us
  matrix products: 17.4 us -> 0 us
  starting transfers between devices: 31.8 us -> 14.7 us
  blocking collectives: 32.5 us -> 19 us
  other arithmetic: 20.6 us -> 8.28 us
  loops' own time: 1.54 us -> 6.75 us
    pallas_call x0 -> x1, Pallas kernels: none -> 39.2 us  [run(): pl.pallas_call(compute, out_shape=jax.ShapeDtypeStruct((count, conduction...]
    all_gather x5 -> x0, blocking collectives: 32.5 us -> none  [the longest x1 7.61 us: shards(): lax.all_gather(orbitals[:, :, :, :valence_count], 'kz', axis=1, tiled=True)]
    unnamed x3 -> x0, waiting for transfers between devices: 30.3 us -> none
    all_to_all x0 -> x1, blocking collectives: none -> 19 us  [run(): terms = lax.all_to_all(partial, axes, 0, 0, tiled=True)]
    dot_general x56 -> x0, matrix products: 17.4 us -> none  [the longest x16 7.19 us: add_block(): lax.dot_general(left_factor, partner_rows, (((0,), (0,)), ((), ())), pref...]
    ppermute x10 -> x7, waiting for transfers between devices: 58.4 us -> 42.7 us  [the longest x4 29 us: swapped(): lax.ppermute(block, axis, [(i, i ^ 1) for i in range(lax.axis_size(axis))])]
    ppermute x10 -> x7, starting transfers between devices: 21.7 us -> 7.42 us  [the longest x3 5.26 us: passed_along(): lax.ppermute(block, 'kp', [(i, (i + PAIR * distance) % size) for i in ran...]
    dynamic_slice x12 -> x0, local copies, waits for them, and re-layouts: 7.31 us -> none  [shards(): lax.map(one_point, (own_valence, own_conduction, valence_first, cond_firs...]
  transfers between devices with their start and end apart: 15 -> 8, of which waited for: 11 -> 5; matrix products, arithmetic and copies ran while one was open for 8% -> 5% of each run, Pallas kernels for 0% -> 0%
where the time goes in v1:
time: 143 us
  waiting for transfers between devices  42.7 us (30%)
  Pallas kernels  39.2 us (27%)
  blocking collectives  19 us (13%)
  starting transfers between devices  14.7 us (10%)
  local copies, waits for them, and re-layouts  10.8 us (8%)
  other arithmetic  8.28 us (6%)
  loops' own time  6.75 us (5%)
    pallas_call x1, Pallas kernels, run(): pl.pallas_call(compute, out_shape=jax.ShapeDtypeStruct((count, conduction...  39.2 us
    ppermute x4, waiting for transfers between devices, swapped(): lax.ppermute(block, axis, [(i, i ^ 1) for i in range(lax.axis_size(axis))])  29 us
    all_to_all x1, blocking collectives, run(): terms = lax.all_to_all(partial, axes, 0, 0, tiled=True)  19 us
    ppermute x3, waiting for transfers between devices, passed_along(): lax.ppermute(block, 'kp', [(i, (i + PAIR * distance) % size) for i in ran...  13.7 us
    all_to_all x1, starting transfers between devices, run(): came = [lax.all_to_all(part, axes, 0, 0, tiled=True) for part in sent]  7.3 us
    another operation x1, loops' own time, shards(): lax.cond(owner_plane[0] == owner_plane[1], functools.partial(run, 2), fun...  6.75 us
    ppermute x3, starting transfers between devices, passed_along(): lax.ppermute(block, 'kp', [(i, (i + PAIR * distance) % size) for i in ran...  5.26 us
  transfers between devices with their start and end apart: 8, of which 5 were waited for; matrix products, arithmetic and copies ran while one was open for 5% of the time, Pallas kernels for 0%

profile of v1, /device:TPU:0, one launch (start us, length us, event | category | flops | bytes accessed | tf_op | source)
XLA Modules:
  0.0 142.9 jit_solution(3555962134146182551)
XLA Ops:
  0.0 1.3 fusion.28
  1.3 1.4 fusion.29
  2.7 2.5 %fusion.10 = (s32[1,32]{1,0:T(1,128)S(1)}, s32[1,32]{1,0:T(1,128)S(1)}) fusion(s32[]{:T(128)} %bitcast.65, s32[]{:T(128)} %bitcast.64, s32[]{:T(128)} %bitcast.67, s32[]{:T(128)} %bitcast.66), kind=kLoop, calls=%fused_computation.108 | loop fusion | flops 2048 | bytes 272 | tf_op jit(solution)/shard_map/add | solution.py:203
  5.2 0.7 and_select_fusion.14
  7.8 134.5 %conditional.1 = (f32[1,1,2,2,1024]{4,3,2,1,0:T(2,128)S(1)}) conditional(s32[]{:T(128)} %bitcast.63, (bf16[1,1,2,64,1024]{4,3,2,1,0:T(8,128)(2,1)}, bf16[1,1,2,2,1024]{4,3,2,1,0:T(2,128)(2,1)}, s32[2]{0:T(128)}, bf16[8,2,256,1024]{3,2,1,0:T(8,128)(2,1)}, s32[]{:T(128)}, /*index=5*/s32[2,32]{1,0:T(2,128)S(1)}, s32[]{:T(128)}, s32[]{:T(128)}, ...), branch_computations={%region_0.2_spmd, %region_2.4_spmd} | conditional | flops 10219773 | bytes 41070916 | solution.py:242
  7.8 1.0 fusion.24
  9.0 0.8 reshape_squeeze.5
  10.2 1.1 pad_maximum_fusion.6
  11.3 7.3 %all-to-all-start.2 = ((bf16[32,144,128]{2,1,0:T(8,128)(2,1)}), bf16[32,144,128]{2,1,0:T(8,128)(2,1)S(1)}, u32[]{:S(2)}, u32[]{:S(2)}) async-start(bf16[32,144,128]{2,1,0:T(8,128)(2,1)} %bitcast.41), calls=%async_computation.2 | async-start | bytes 2359296 | tf_op jit(solution)/shard_map/cond/branch_1_fun/all_to_all | solution.py:212
  23.1 1.3 dynamic-slice_bitcast_fusion.11
  24.4 1.8 %collective-permute-start.8 = (bf16[2,128,1024]{2,1,0:T(8,128)(2,1)S(1)}, bf16[2,128,1024]{2,1,0:T(8,128)(2,1)S(1)}, u32[]{:S(2)}, u32[]{:S(2)}) collective-permute-start(bf16[2,128,1024]{2,1,0:T(8,128)(2,1)S(1)} %get-tuple-element.113), channel_id=1, source_target_pairs={{0,4},{4,0},{8,12},{12,8},{16,20},{20,16},{24,28},{28,24},{1,5},{5... | collective-permute-start | bytes 1572872 | tf_op jit(solution)/shard_map/cond/branch_1_fun/ppermute | solution.py:17
  28.5 16.8 %collective-permute-done.8 = bf16[2,128,1024]{2,1,0:T(8,128)(2,1)S(1)} collective-permute-done((bf16[2,128,1024]{2,1,0:T(8,128)(2,1)S(1)}, bf16[2,128,1024]{2,1,0:T(8,128)(2,1)S(1)}, u32[]{:S(2)}, u32[]{:S(2)}) %collective-permute-start.8) | collective-permute-done | bytes 524320 | tf_op jit(solution)/shard_map/cond/branch_1_fun/ppermute | solution.py:17
  45.2 11.7 %collective-permute-done.9 = bf16[2,128,1024]{2,1,0:T(8,128)(2,1)S(1)} collective-permute-done((bf16[2,128,1024]{2,1,0:T(8,128)(2,1)S(1)}, bf16[2,128,1024]{2,1,0:T(8,128)(2,1)S(1)}, u32[]{:S(2)}, u32[]{:S(2)}) %collective-permute-start.9) | collective-permute-done | bytes 524320 | tf_op jit(solution)/shard_map/cond/branch_1_fun/ppermute | solution.py:17
  56.9 1.6 %fusion = (bf16[1,2,128,1024]{3,2,1,0:T(8,128)(2,1)S(1)}, bf16[1,2,128,1024]{3,2,1,0:T(8,128)(2,1)S(1)}) fusion(bf16[2,128,1024]{2,1,0:T(8,128)(2,1)S(1)} %collective-permute-done.9, bf16[8,2,256,1024]{3,2,1,0:T(8,128)(2,1)} %get-tuple-element.58, s32[]{:T(128)S(6)} %select_n.275, s32[]{:T(128)S(6)} %select_n.271, pred[]{:T(512)S(6)} %eq.45, ...), kind=kLoop, calls=%fused_computation.50 | loop fusion | flops 524288 | bytes 3145742 | tf_op jit(solution)/shard_map/cond/branch_1_fun/stack | solution.py:83
  58.8 1.4 %collective-permute-start.10 = (bf16[2,2,128,256]{3,2,1,0:T(8,128)(2,1)S(1)}, bf16[2,2,128,256]{3,2,1,0:T(8,128)(2,1)S(1)}, u32[]{:S(2)}, u32[]{:S(2)}) collective-permute-start(bf16[2,2,128,256]{3,2,1,0:T(8,128)(2,1)S(1)} %pad_maximum_fusion.8), channel_id=1, source_target_pairs={{0,8},{4,12},{8,16},{12,20},{16,24},{20,28},{24,0},{28,4},{1,9},{5... | collective-permute-start | bytes 786440 | tf_op jit(solution)/shard_map/cond/branch_1_fun/ppermute | solution.py:22
  60.3 2.3 %collective-permute-start.11 = (bf16[2,2,128,256]{3,2,1,0:T(8,128)(2,1)S(1)}, bf16[2,2,128,256]{3,2,1,0:T(8,128)(2,1)}, u32[]{:S(2)}, u32[]{:S(2)}) collective-permute-start(bf16[2,2,128,256]{3,2,1,0:T(8,128)(2,1)S(1)} %pad_maximum_fusion.9), channel_id=1, source_target_pairs={{0,16},{4,20},{8,24},{12,28},{16,0},{20,4},{24,8},{28,12},{1,17},{... | collective-permute-start | bytes 786440 | tf_op jit(solution)/shard_map/cond/branch_1_fun/ppermute | solution.py:22
  62.7 1.5 %collective-permute-start.12 = (bf16[2,2,128,256]{3,2,1,0:T(8,128)(2,1)S(1)}, bf16[2,2,128,256]{3,2,1,0:T(8,128)(2,1)}, u32[]{:S(2)}, u32[]{:S(2)}) collective-permute-start(bf16[2,2,128,256]{3,2,1,0:T(8,128)(2,1)S(1)} %pad_maximum_fusion.10), channel_id=1, source_target_pairs={{0,24},{4,28},{8,0},{12,4},{16,8},{20,12},{24,16},{28,20},{1,25},{... | collective-permute-start | bytes 786440 | tf_op jit(solution)/shard_map/cond/branch_1_fun/ppermute | solution.py:22
  64.2 0.9 fusion.23
  66.6 3.4 %collective-permute-done.10 = bf16[2,2,128,256]{3,2,1,0:T(8,128)(2,1)S(1)} collective-permute-done((bf16[2,2,128,256]{3,2,1,0:T(8,128)(2,1)S(1)}, bf16[2,2,128,256]{3,2,1,0:T(8,128)(2,1)S(1)}, u32[]{:S(2)}, u32[]{:S(2)}) %collective-permute-start.10) | collective-permute-done | bytes 262176 | tf_op jit(solution)/shard_map/cond/branch_1_fun/ppermute | solution.py:22
  69.9 10.3 %collective-permute-done.11 = bf16[2,2,128,256]{3,2,1,0:T(8,128)(2,1)} collective-permute-done((bf16[2,2,128,256]{3,2,1,0:T(8,128)(2,1)S(1)}, bf16[2,2,128,256]{3,2,1,0:T(8,128)(2,1)}, u32[]{:S(2)}, u32[]{:S(2)}) %collective-permute-start.11) | collective-permute-done | bytes 262176 | tf_op jit(solution)/shard_map/cond/branch_1_fun/ppermute | solution.py:22
  80.3 1.2 pad_maximum_fusion.7
  81.6 0.7 pad_maximum_fusion.11.screen_ref
  83.7 39.2 %branch_1_fun.1 = bf16[32,32,128]{2,1,0:T(8,128)(2,1)} custom-call(s32[1]{0:T(128)} %bitcast.34.core_ref, s32[2,32]{1,0:T(2,128)S(1)} %copy-done.10, bf16[32,64,128]{2,1,0:T(8,128)(2,1)} %copy-done.1, bf16[32,64,128]{2,1,0:T(8,128)(2,1)} %copy-done.3, bf16[32,64,128]{2,1,0:T(8,128)(2,1)} %get-tuple-element.114.cond_ref, bf16[32,16,128]{2,1,0:T(8,128)(2,1)} %copy-done.4, ...), custom_call_target="tpu_custom_call" | custom-call | tf_op jit(solution)/shard_map/cond/branch_1_fun/pallas_call | solution.py:225
  123.0 19.0 %all_to_all.17 = bf16[32,32,128]{2,1,0:T(8,128)(2,1)S(1)} all-to-all(bf16[32,32,128]{2,1,0:T(8,128)(2,1)} %branch_1_fun.1), channel_id=1, replica_groups=mesh['kp'=8,'kz'=4] {'kp','kz'}, dimensions={0} | all-to-all | bytes 524288 | tf_op jit(solution)/shard_map/cond/branch_1_fun/all_to_all | solution.py:236
  (50 shorter events, 5.5 us)
Async XLA Ops:
  7.8 3.6 %copy-start.9 = (s32[2,32]{1,0:T(2,128)}, s32[2,32]{1,0:T(2,128)S(1)}, u32[]{:S(2)}) copy-start(s32[2,32]{1,0:T(2,128)S(1)} %get-tuple-element.39.own_ref) | copy-start | bytes 772 | tf_op jit(solution)/shard_map/cond
  10.2 8.5 %copy-start.12 = (s32[2]{0:T(128)S(1)}, s32[2]{0:T(128)}, u32[]{:S(2)}) copy-start(s32[2]{0:T(128)} %get-tuple-element.42) | copy-start | bytes 28 | tf_op jit(solution)/shard_map/cond
  11.3 52.9 %all-to-all-start.2 = ((bf16[32,144,128]{2,1,0:T(8,128)(2,1)}), bf16[32,144,128]{2,1,0:T(8,128)(2,1)S(1)}, u32[]{:S(2)}, u32[]{:S(2)}) async-start(bf16[32,144,128]{2,1,0:T(8,128)(2,1)} %bitcast.41), calls=%async_computation.2 | async-start | bytes 2359296 | tf_op jit(solution)/shard_map/cond/branch_1_fun/all_to_all | solution.py:212
  24.4 20.8 %collective-permute-start.8 = (bf16[2,128,1024]{2,1,0:T(8,128)(2,1)S(1)}, bf16[2,128,1024]{2,1,0:T(8,128)(2,1)S(1)}, u32[]{:S(2)}, u32[]{:S(2)}) collective-permute-start(bf16[2,128,1024]{2,1,0:T(8,128)(2,1)S(1)} %get-tuple-element.113), channel_id=1, source_target_pairs={{0,4},{4,0},{8,12},{12,8},{16,20},{20,16},{24,28},{28,24},{1,5},{5... | collective-permute-start | bytes 1572872 | tf_op jit(solution)/shard_map/cond/branch_1_fun/ppermute | solution.py:17
  26.3 30.7 %collective-permute-start.9 = (bf16[2,128,1024]{2,1,0:T(8,128)(2,1)S(1)}, bf16[2,128,1024]{2,1,0:T(8,128)(2,1)S(1)}, u32[]{:S(2)}, u32[]{:S(2)}) collective-permute-start(bf16[2,128,1024]{2,1,0:T(8,128)(2,1)S(1)} %get-tuple-element.112), channel_id=1, source_target_pairs={{0,4},{4,0},{8,12},{12,8},{16,20},{20,16},{24,28},{28,24},{1,5},{5... | collective-permute-start | bytes 1572872 | tf_op jit(solution)/shard_map/cond/branch_1_fun/ppermute | solution.py:17
  58.8 11.1 %collective-permute-start.10 = (bf16[2,2,128,256]{3,2,1,0:T(8,128)(2,1)S(1)}, bf16[2,2,128,256]{3,2,1,0:T(8,128)(2,1)S(1)}, u32[]{:S(2)}, u32[]{:S(2)}) collective-permute-start(bf16[2,2,128,256]{3,2,1,0:T(8,128)(2,1)S(1)} %pad_maximum_fusion.8), channel_id=1, source_target_pairs={{0,8},{4,12},{8,16},{12,20},{16,24},{20,28},{24,0},{28,4},{1,9},{5... | collective-permute-start | bytes 786440 | tf_op jit(solution)/shard_map/cond/branch_1_fun/ppermute | solution.py:22
  60.3 20.0 %collective-permute-start.11 = (bf16[2,2,128,256]{3,2,1,0:T(8,128)(2,1)S(1)}, bf16[2,2,128,256]{3,2,1,0:T(8,128)(2,1)}, u32[]{:S(2)}, u32[]{:S(2)}) collective-permute-start(bf16[2,2,128,256]{3,2,1,0:T(8,128)(2,1)S(1)} %pad_maximum_fusion.9), channel_id=1, source_target_pairs={{0,16},{4,20},{8,24},{12,28},{16,0},{20,4},{24,8},{28,12},{1,17},{... | collective-permute-start | bytes 786440 | tf_op jit(solution)/shard_map/cond/branch_1_fun/ppermute | solution.py:22
  62.7 17.6 %collective-permute-start.12 = (bf16[2,2,128,256]{3,2,1,0:T(8,128)(2,1)S(1)}, bf16[2,2,128,256]{3,2,1,0:T(8,128)(2,1)}, u32[]{:S(2)}, u32[]{:S(2)}) collective-permute-start(bf16[2,2,128,256]{3,2,1,0:T(8,128)(2,1)S(1)} %pad_maximum_fusion.10), channel_id=1, source_target_pairs={{0,24},{4,28},{8,0},{12,4},{16,8},{20,12},{24,16},{28,20},{1,25},{... | collective-permute-start | bytes 786440 | tf_op jit(solution)/shard_map/cond/branch_1_fun/ppermute | solution.py:22
  65.2 17.7 %copy-start.1 = (bf16[32,64,128]{2,1,0:T(8,128)(2,1)}, bf16[32,64,128]{2,1,0:T(8,128)(2,1)S(1)}, u32[]{:S(2)}) copy-start(bf16[32,64,128]{2,1,0:T(8,128)(2,1)S(1)} %get-tuple-element.115.near_ref) | copy-start | bytes 1572868 | tf_op jit(solution)/shard_map/cond
  65.2 18.6 %copy-start.10 = (s32[2,32]{1,0:T(2,128)S(1)}, s32[2,32]{1,0:T(2,128)}, u32[]{:S(2)}) copy-start(s32[2,32]{1,0:T(2,128)} %copy-done.9) | copy-start | bytes 772 | tf_op jit(solution)/shard_map/cond
  65.2 17.7 %collective-permute-start.6 = (bf16[32,64,128]{2,1,0:T(8,128)(2,1)S(1)}, bf16[32,64,128]{2,1,0:T(8,128)(2,1)S(1)}, u32[]{:S(2)}, u32[]{:S(2)}) collective-permute-start(bf16[32,64,128]{2,1,0:T(8,128)(2,1)S(1)} %get-tuple-element.115.near_ref), channel_id=1, source_target_pairs={{0,1},{1,0},{2,3},{3,2},{4,5},{5,4},{6,7},{7,6},{8,9},{9,8},{10,11... | collective-permute-start | bytes 1572872 | tf_op jit(solution)/shard_map/cond/branch_1_fun/ppermute | solution.py:17
  81.5 1.4 %copy-start.4 = (bf16[32,16,128]{2,1,0:T(8,128)(2,1)}, bf16[32,16,128]{2,1,0:T(8,128)(2,1)S(1)}, u32[]{:S(2)}) copy-start(bf16[32,16,128]{2,1,0:T(8,128)(2,1)S(1)} %slice.115.tri_near_ref) | copy-start | bytes 393220 | tf_op jit(solution)/shard_map/cond
  81.5 1.4 collective-permute-start.7
  82.9 0.7 copy-start.6
  82.9 0.8 copy-start.3
  142.3 0.6 copy-start.8
